TPU v7x, 256 devices: a whole 4x4x8 slice. The times are simulated.
256 devices in a mesh: rows: 64 (over z, y, core), cols: 4 (over x).
Axes of the slice: x: 4, y: 4, z: 8, core: 2. Of those that a mesh axis runs over, the one named last changes fastest.
Arguments:
- mutant_factors: bfloat16 [524288, 128], P(('rows', 'cols')), may hold values from -0.019334951 to 0.019334951
- test_factors: float32 [32768, 128], P('rows'), may hold values from -6 to 6
- weights: bfloat16 [64, 4, 28, 256, 256], P('rows', 'cols'), may hold values from 1 to 100
- pattern: int32 [64, 4, 28, 256, 256], P('rows', 'cols'), may hold values 0 or 1
- tile_block: int32 [64, 4, 28], P('rows', 'cols'), may hold values from 0 to 1
- hub_pick: int32 [64, 4, 8], P('rows', 'cols'), may hold values from 0 to 7
- hub_blocks: int32 [8], replicated, may hold values from 0 to 2047, as said below
- tail_req: int32 [64, 4, 64, 80], P('rows', 'cols'), may hold values from 0 to 2047
- tail_pick: int32 [64, 4, 5120], P('rows', 'cols'), may hold values from 0 to 5119, each once within a row
Outputs:
- test_solution: float32 [32768, 128], P(('rows', 'cols'))
- test_residual: float32 [32768, 128], P(('rows', 'cols'))
Inputs may be any that keep to these rules, and one draw needn't show every extreme that they name: `hub_blocks`: the 8 hub blocks are distinct, and the last mutant block is always one of them. tail_req[r, c, o, j] is a row among the 2048 mutant rows of the device at rows index o and cols index c. `tail_pick`: each device's list is a permutation.
All inputs are finite; a program needn't handle non-finite values. No bound on the sum of `pattern` on one device may be relied on, other than what follows from the above.
Results may differ from a plain program's by a relative error of at most 0.003.
Values may be sent and summed in bfloat16 or wider, within the bound.
A program may use at most 128 MiB of HBM per device.

v0:
```python
import jax
import jax.numpy as jnp
from jax import lax
from jax.sharding import PartitionSpec as P

ITERS = 2


ridge = 0.1
tiny = 1e-06
highest = lax.Precision.HIGHEST


def from_root(shard, axis, root):
    mine = lax.axis_index(axis) == root
    return lax.psum(jnp.where(mine, shard, jnp.zeros_like(shard)), axis)


def per_device(
    mutant_factors,
    test_factors,
    weights,
    pattern,
    tile_block,
    hub_pick,
    hub_blocks,
    tail_req,
    tail_pick,
):
    mutant_rows, factor_width = mutant_factors.shape
    tile_size = weights.shape[-1]
    tile_count = weights.shape[2]
    hub_tile_count = hub_pick.shape[2]
    tail_count = tile_count - hub_tile_count
    hub_count = hub_blocks.shape[0]
    full_rows = test_factors.shape[0]
    block_count = full_rows // tile_size
    col_count = lax.axis_size("cols")
    share_rows = full_rows // col_count
    blocks_here = mutant_rows // tile_size
    local_gram = lax.dot_general(
        mutant_factors, mutant_factors, (((0,), (0,)), ((), ())), preferred_element_type=jnp.float32
    )
    gram_matrix = lax.psum(local_gram, ("rows", "cols"))
    offsets = hub_blocks % blocks_here * tile_size
    owners = hub_blocks // blocks_here
    fetched = []
    for hub_index in range(hub_count):
        own_block = lax.dynamic_slice_in_dim(mutant_factors, offsets[hub_index], tile_size, 0)
        fetched.append(from_root(own_block, ("rows", "cols"), owners[hub_index]))
    hub_rows = jnp.stack(fetched)
    requests = tail_req[0, 0]
    sent_rows = jnp.take(
        mutant_factors,
        lax.all_to_all(requests, "rows", split_axis=0, concat_axis=0, tiled=True),
        axis=0,
    )
    received = lax.all_to_all(sent_rows, "rows", split_axis=0, concat_axis=0, tiled=True)
    tail_tiles = jnp.take(received.reshape(-1, factor_width), tail_pick[0, 0], axis=0)
    tail_tiles = tail_tiles.reshape(tail_count, tile_size, factor_width)
    hub_select = (hub_pick[0, 0][:, None] == jnp.arange(hub_count)[None, :]).astype(jnp.bfloat16)
    hub_tiles = jnp.einsum(
        "nh,htk->ntk", hub_select, hub_rows, preferred_element_type=jnp.float32
    ).astype(jnp.bfloat16)
    tile_factors = jnp.concatenate([hub_tiles, tail_tiles], axis=0)
    tile_weights = weights[0, 0]
    tile_pattern = pattern[0, 0]
    eff_weight = tile_weights * tile_pattern.astype(jnp.bfloat16)
    confidence = (
        tile_pattern.astype(jnp.float32) * (1.0 + tile_weights.astype(jnp.float32))
    ).astype(jnp.bfloat16)
    block_select = (tile_block[0, 0][:, None] == jnp.arange(block_count)[None, :]).astype(
        jnp.float32
    )
    select_half = block_select.astype(jnp.bfloat16)

    def spread(per_tile):
        return jnp.einsum("nb,ntk->btk", block_select, per_tile, precision=highest).reshape(
            full_rows, factor_width
        )

    def tile_terms(vector):
        pieces = jnp.einsum(
            "nb,btk->ntk",
            select_half,
            vector.reshape(block_count, tile_size, factor_width),
            preferred_element_type=jnp.float32,
        ).astype(jnp.bfloat16)
        scores = jnp.einsum(
            "ntk,nmk->ntm", pieces, tile_factors, preferred_element_type=jnp.float32
        )
        weighted = (scores * eff_weight).astype(jnp.bfloat16)
        return spread(
            jnp.einsum("ntm,nmk->ntk", weighted, tile_factors, preferred_element_type=jnp.float32)
        )

    right_terms = spread(
        jnp.einsum("ntm,nmk->ntk", confidence, tile_factors, preferred_element_type=jnp.float32)
    )
    col_index = lax.axis_index("cols")
    solution = test_factors

    def reduce_terms(terms):
        return lax.psum(terms, "cols")

    def operator_rest(vector):
        return jnp.dot(vector, gram_matrix, precision=highest) + ridge * vector

    residual = reduce_terms(
        right_terms - tile_terms(test_factors.astype(jnp.bfloat16))
    ) - operator_rest(solution)
    direction = residual
    norm_now = jnp.sum(residual * residual, axis=1, keepdims=True)
    for iteration in range(ITERS):
        applied = reduce_terms(tile_terms(direction.astype(jnp.bfloat16))) + operator_rest(
            direction
        )
        step_size = norm_now / (jnp.sum(direction * applied, axis=1, keepdims=True) + tiny)
        solution = solution + step_size * direction
        residual = residual - step_size * applied
        norm_next = jnp.sum(residual * residual, axis=1, keepdims=True)
        direction = residual + norm_next / (norm_now + tiny) * direction
        norm_now = norm_next
    solution = lax.dynamic_slice_in_dim(solution, col_index * share_rows, share_rows, 0)
    residual = lax.dynamic_slice_in_dim(residual, col_index * share_rows, share_rows, 0)
    return (solution, residual)


def solution(mesh):
    in_specs = (
        P(("rows", "cols"), None),
        P("rows", None),
        P("rows", "cols", None, None, None),
        P("rows", "cols", None, None, None),
        P("rows", "cols", None),
        P("rows", "cols", None),
        P(),
        P("rows", "cols", None, None),
        P("rows", "cols", None),
    )
    out_specs = (P(("rows", "cols"), None), P(("rows", "cols"), None))
    return jax.shard_map(
        per_device, mesh=mesh, in_specs=in_specs, out_specs=out_specs, check_vma=False
    )
```

profile of v0, /device:TPU:8, one launch (start us, length us, event | category | flops | bytes accessed | tf_op | source)
XLA Modules:
  0.0 736.1 jit_solution(5622951508304491674)
XLA Ops:
  7.2 0.7 and_select_fusion.1
  7.9 0.7 fusion.61
  28.6 1.4 select_bitcast_fusion
  30.1 0.8 copy.240
  30.8 0.8 copy.239
  31.6 0.7 copy.238
  32.3 0.7 copy.237
  33.1 0.8 copy.236
  33.8 0.8 copy.235
  34.6 0.7 copy.234
  35.3 0.8 copy.233
  36.1 12.1 %all-to-all-start = ((s32[64,1,80]{2,1,0:T(1,128)}), s32[64,1,80]{2,1,0:T(1,128)S(1)}, u32[]{:S(2)}, u32[]{:S(2)}) async-start(s32[64,1,80]{2,1,0:T(1,128)} %bitcast.29), calls=%async_computation | async-start | bytes 65536 | tf_op jit(solution)/shard_map/all_to_all | solution.py:55
  48.2 0.0 all-reduce.9.cloned.1.call-start
  48.3 1.0 fusion.64
  49.3 0.5 broadcast.142
  49.8 0.7 reduce.3
  50.5 6.2 all-to-all-done
  56.8 0.1 reshape.148
  56.9 15.1 %gather_fusion = bf16[5120,128]{1,0:T(8,128)(2,1)S(1)} fusion(bf16[2048,128]{1,0:T(8,128)(2,1)S(1)} %copy-done, s32[5120]{0:T(1024)S(1)} %broadcast_clamp_fusion.1), kind=kCustom, calls=%fused_computation | custom fusion | bytes 2641920 | tf_op jit(solution)/shard_map/jit(_take)/gather | solution.py:53
  72.0 2.2 broadcast_select_fusion
  74.2 5.7 all-to-all-start.1
  79.9 0.0 all-reduce.7.cloned.1.call-start
  80.1 2.1 convolution_convert_fusion.2
  82.2 6.5 convert_multiply_fusion.3
  88.7 212.9 %all-reduce.15.cloned.1.call-done = (bf16[1,256,128]{2,0,1:T(2,128)(2,1)}, bf16[1,256,128]{2,0,1:T(2,128)(2,1)}, bf16[1,256,128]{2,0,1:T(2,128)(2,1)}, bf16[1,25...) async-done(((bf16[1,256,128]{2,0,1:T(2,128)(2,1)}, ...) | async-done | bytes 524304 | tf_op jit(solution)/shard_map/psum | solution.py:16
  301.6 2.9 stack.35
  304.6 0.4 convolution_convert_fusion.3
  304.9 0.9 copy.241
  305.8 15.1 %gather_fusion.1 = bf16[5120,128]{1,0:T(8,128)(2,1)S(1)} fusion(bf16[5120,128]{1,0:T(8,128)(2,1)S(1)} %bitcast.112, s32[5120]{0:T(1024)S(1)} %broadcast_clamp_fusion), kind=kCustom, calls=%fused_computation.1 | custom fusion | bytes 2641920 | tf_op jit(solution)/shard_map/jit(_take)/gather | solution.py:59
  320.9 1.2 broadcast_select_fusion.1
  322.2 7.5 %fusion.8 = f32[28,256,128]{2,1,0:T(8,128)} fusion(bf16[1,1,28,256,256]{4,3,2,1,0:T(8,128)(2,1)} %param.11, s32[1,1,28,256,256]{4,3,2,1,0:T(8,128)} %param.12, bf16[20,256,128]{2,1,0:T(8,128)(2,1)S(1)} %broadcast_select_fusion.1, bf16[8,256,128]{2,1,0:T(8,128)(2,1)S(1)} %copy-done.3), kind=kOutput, calls=%fused_computation.14 | convolution fusion | flops 479854592 | bytes 16515072 | tf_op jit(solution)/shard_map/ntm,nmk->ntk/dot_general | solution.py:98
  329.7 6.9 fusion.14
  336.6 5.5 fusion.3
  342.1 3.5 fusion.32
  345.7 0.8 copy.247
  346.5 0.3 all-reduce.11.cloned.1.call-start
  346.8 0.1 copy.254
  346.9 197.3 %all-reduce.9.cloned.1.call-done = f32[128,128]{1,0:T(8,128)} async-done(((f32[128,128]{1,0:T(8,128)}), f32[128,128]{1,0:T(8,128)}) %all-reduce.9.cloned.1.call-update) | async-done | bytes 65552 | tf_op jit(solution)/shard_map/psum | solution.py:44
  544.2 46.4 %all-reduce.7.cloned.1.call-done = f32[512,128]{0,1:T(8,128)} async-done(((f32[512,128]{0,1:T(8,128)}), f32[512,128]{0,1:T(8,128)}) %all-reduce.7.cloned.1.call-update) | async-done | bytes 262160 | tf_op jit(solution)/shard_map/psum | solution.py:104
  590.7 1.4 fusion.63
  592.1 0.1 copy.249
  592.3 2.2 convolution_convert_fusion.1
  594.4 6.8 fusion.12
  601.3 5.5 copy.261
  606.8 3.6 fusion.46
  610.4 0.7 copy.268
  611.1 0.0 all-reduce.13.cloned.1.call-start
  611.2 47.4 %all-reduce.11.cloned.1.call-done = f32[512,128]{0,1:T(8,128)} async-done(((f32[512,128]{0,1:T(8,128)}), f32[512,128]{0,1:T(8,128)}) %all-reduce.11.cloned.1.call-update) | async-done | bytes 262160 | tf_op jit(solution)/shard_map/psum | solution.py:104
  658.6 1.4 multiply_reduce_fusion.2
  660.0 0.1 multiply_reduce_fusion.1
  660.1 0.1 fusion.60
  660.2 0.1 copy.255
  660.3 2.2 convolution_convert_fusion
  662.5 6.8 fusion.10
  669.3 5.5 copy.264
  674.8 3.6 fusion.44
  678.4 0.7 copy.269
  679.2 0.1 dynamic-slice
  679.3 47.3 %all-reduce.13.cloned.1.call-done = f32[512,128]{0,1:T(8,128)} async-done(((f32[512,128]{0,1:T(8,128)}), f32[512,128]{0,1:T(8,128)}) %all-reduce.13.cloned.1.call-update) | async-done | bytes 262160 | tf_op jit(solution)/shard_map/psum | solution.py:104
  726.6 1.4 multiply_reduce_fusion
  728.0 0.1 dynamic-slice.1
  728.1 0.1 dynamic-slice_subtract_fusion
  728.1 0.7 copy.260
  728.9 0.7 copy.259
  (39 shorter events, 0.4 us)
Async XLA Ops:
  7.2 41.1 %copy-start = (bf16[2048,128]{1,0:T(8,128)(2,1)S(1)}, bf16[2048,128]{1,0:T(8,128)(2,1)}, u32[]{:S(2)}) copy-start(bf16[2048,128]{1,0:T(8,128)(2,1)} %param.9) | copy-start | bytes 1572868
  7.2 294.4 %all-reduce.15.cloned.1.call-start = ((), (), s32[]{:S(2)}) async-start(), calls=%async_computation.6 | async-start | bytes 2097152 | tf_op jit(solution)/shard_map/psum | solution.py:16
  30.0 19.8 %copy-start.6 = (s32[1,1,5120]{2,1,0:T(1,128)S(1)}, s32[1,1,5120]{2,1,0:T(1,128)}, u32[]{:S(2)}) copy-start(s32[1,1,5120]{2,1,0:T(1,128)} %param.17) | copy-start | bytes 61444
  36.1 20.6 %all-to-all-start = ((s32[64,1,80]{2,1,0:T(1,128)}), s32[64,1,80]{2,1,0:T(1,128)S(1)}, u32[]{:S(2)}, u32[]{:S(2)}) async-start(s32[64,1,80]{2,1,0:T(1,128)} %bitcast.29), calls=%async_computation | async-start | bytes 65536 | tf_op jit(solution)/shard_map/all_to_all | solution.py:55
  48.2 496.0 %all-reduce.9.cloned.1.call-start = ((), (), s32[]{:S(2)}) async-start(), calls=%async_computation.3 | async-start | bytes 131072 | tf_op jit(solution)/shard_map/psum | solution.py:44
  72.0 8.0 %copy-start.2 = (f32[512,128]{1,0:T(8,128)S(1)}, f32[512,128]{1,0:T(8,128)}, u32[]{:S(2)}) copy-start(f32[512,128]{1,0:T(8,128)} %param.10) | copy-start | bytes 786436
  74.2 5.9 copy-start.7
  74.2 231.6 %all-to-all-start.1 = ((bf16[64,80,128]{2,1,0:T(8,128)(2,1)}), bf16[64,80,128]{2,1,0:T(8,128)(2,1)S(1)}, u32[]{:S(2)}, u32[]{:S(2)}) async-start(bf16[64,80,128]{2,1,0:T(8,128)(2,1)} %broadcast_select_fusion), calls=%async_computation.1 | async-start | bytes 2621440 | tf_op jit(solution)/shard_map/all_to_all | solution.py:58
  79.9 510.7 %all-reduce.7.cloned.1.call-start = ((), (), s32[]{:S(2)}) async-start(), calls=%async_computation.2 | async-start | bytes 524288 | tf_op jit(solution)/shard_map/psum | solution.py:104
  82.2 222.4 %copy-start.8 = (s32[1,1,8]{2,1,0:T(1,128)S(1)}, s32[1,1,8]{2,1,0:T(1,128)}, u32[]{:S(2)}) copy-start(s32[1,1,8]{2,1,0:T(1,128)} %param.14) | copy-start | bytes 100
  320.9 1.2 copy-start.3
  322.2 7.5 %copy-start.4 = (bf16[8,256,128]{2,1,0:T(8,128)(2,1)S(1)}, bf16[8,256,128]{2,1,0:T(8,128)(2,1)}, u32[]{:S(2)}) copy-start(bf16[8,256,128]{2,1,0:T(8,128)(2,1)} %copy.241) | copy-start | bytes 1572868
  336.6 5.5 copy-start.1
  346.5 312.1 %all-reduce.11.cloned.1.call-start = ((), (), s32[]{:S(2)}) async-start(), calls=%async_computation.4 | async-start | bytes 524288 | tf_op jit(solution)/shard_map/psum | solution.py:104
  606.8 51.8 %copy-start.5 = (f32[128,128]{1,0:T(8,128)S(1)}, f32[128,128]{1,0:T(8,128)}, u32[]{:S(2)}) copy-start(f32[128,128]{1,0:T(8,128)} %all-reduce.9.cloned.1.call-done) | copy-start | bytes 196612
  611.1 115.4 %all-reduce.13.cloned.1.call-start = ((), (), s32[]{:S(2)}) async-start(), calls=%async_computation.5 | async-start | bytes 524288 | tf_op jit(solution)/shard_map/psum | solution.py:104
Sparse Core Ops, SparseCore 0:
  36.2 265.3 all-reduce.14
  308.6 235.5 all-reduce.8
  546.7 43.9 all-reduce.6
  611.3 47.2 all-reduce.10
  679.3 47.2 all-reduce.12
where the time goes:
time: 737 us; the launch traced here: 736 us
  waiting for transfers between devices  558 us (76%)
  local copies, waits for them, and re-layouts  56.8 us (8%)
  matrix products  56.3 us (8%)
  between operations  34.1 us (5%)
  starting transfers between devices  18.2 us (2%)
  other arithmetic  13 us (2%)
    psum x1, waiting for transfers between devices, from_root(): return lax.psum(jnp.where(mine, shard, jnp.zeros_like(shard)), axis)  213 us
    psum x1, waiting for transfers between devices, per_device(): gram_matrix = lax.psum(local_gram, ('rows', 'cols'))  197 us
    psum x3, waiting for transfers between devices, reduce_terms(): return lax.psum(terms, 'cols')  141 us
    dot_general x3, matrix products, tile_terms(): jnp.einsum('ntm,nmk->ntk', weighted, tile_factors, preferred_element_type...  20.5 us
    dot_general x4, matrix products, spread(): jnp.einsum('nb,ntk->btk', block_select, per_tile, precision=highest)  16.3 us
    gather x1, local copies, waits for them, and re-layouts, per_device(): jnp.take(mutant_factors, lax.all_to_all(requests, 'rows', split_axis=0, c...  15.1 us
    gather x1, local copies, waits for them, and re-layouts, per_device(): jnp.take(received.reshape(-1, factor_width), tail_pick[0, 0], axis=0)  15.1 us
  transfers between devices with their start and end apart: 7, of which 6 were waited for; matrix products, arithmetic and copies ran while one was open for 10% of the time, Pallas kernels for 0%

commit v1 on v0

v1 whole, which is shorter than its diff:
```python
import functools

import jax
import jax.numpy as jnp
from jax import lax
from jax.experimental import pallas as pl
from jax.experimental.pallas import tpu as pltpu
from jax.sharding import PartitionSpec as P

ITERS = 2

ridge = 0.1
tiny = 1e-06
highest = lax.Precision.HIGHEST
f32 = jnp.float32
bf16 = jnp.bfloat16


def fold(a, b):
    return lax.dot_general(a, b, (((0,), (0,)), ((), ())), preferred_element_type=f32)


def across(a, b):
    return lax.dot_general(a, b, (((1,), (1,)), ((), ())), preferred_element_type=f32)


def plain(a, b):
    return jnp.dot(a, b, preferred_element_type=f32)


def remote(src, dst, send_sem, recv_sem, row, col):
    return pltpu.make_async_remote_copy(
        src_ref=src,
        dst_ref=dst,
        send_sem=send_sem,
        recv_sem=recv_sem,
        device_id=(row, col),
        device_id_type=pl.DeviceIdType.MESH,
    )


def drain(ref, sem):
    pltpu.make_async_copy(ref, ref, sem).wait()


def kernel(
    dims,
    mutants_h,
    start_h,
    weights_h,
    pattern_h,
    requests_h,
    pick_h,
    block_s,
    hub_pick_s,
    hub_block_s,
    solution_ref,
    residual_ref,
    mutants,
    mutants32,
    start,
    weights,
    pattern,
    confidence,
    requests,
    pick_s,
    asked_out,
    asked_in,
    asked_s,
    rows32,
    answers,
    received,
    tail32,
    tile32,
    tail,
    hub_mine,
    hub_x,
    hub_xsum,
    hub_y,
    hub_ysum,
    hub_z,
    hub_share,
    hub_all,
    gram_mine,
    gram_x,
    gram_xsum,
    gram_y,
    gram_ysum,
    gram_z,
    gram_zsum,
    gram_all,
    start_half,
    direction_half,
    terms,
    terms_in,
    local_sem,
    asked_sem,
    answer_send,
    answer_recv,
    hub_send,
    hub_recv,
    gram_send,
    gram_recv,
    terms_send,
    terms_recv,
    dir_send,
    dir_recv,
):
    n_rows, n_cols, planes, ring, cap, tile, tiles, hub_tiles, hubs = dims
    row = lax.axis_index("rows")
    col = lax.axis_index("cols")
    z = lax.div(row, ring)
    yc = lax.rem(row, ring)
    tail_tiles = tiles - hub_tiles

    def near_x(k):
        return lax.rem(col + k, n_cols)

    def near_y(k):
        return lax.rem(yc + k, ring)

    def near_z(k):
        return lax.rem(z + k, planes)

    def partner(i):
        k = lax.rem(i, planes)
        half = lax.div(k + 1, 2)
        dz = planes // 2 + half * (1 - 2 * lax.rem(k, 2))
        dy = lax.div(i, planes) + 1
        return lax.rem(z + dz, planes) * ring + lax.rem(yc + dy, ring)

    dir_words = (n_cols - 1) * (start.shape[0] // n_cols) // hub_ysum.shape[0]

    local = [
        pltpu.make_async_copy(requests_h, requests, local_sem.at[0]),
        pltpu.make_async_copy(mutants_h, mutants, local_sem.at[1]),
        pltpu.make_async_copy(pick_h, pick_s, local_sem.at[2]),
        pltpu.make_async_copy(start_h, start, local_sem.at[3]),
        pltpu.make_async_copy(weights_h, weights, local_sem.at[4]),
        pltpu.make_async_copy(pattern_h, pattern, local_sem.at[5]),
    ]
    for copy in local:
        copy.start()

    barrier = pltpu.get_barrier_semaphore()

    def greet(i, carry):
        pl.semaphore_signal(
            barrier, inc=1, device_id=(partner(i), col), device_id_type=pl.DeviceIdType.MESH
        )
        return carry

    lax.fori_loop(0, n_rows - 1, greet, 0)
    for k in range(1, n_cols):
        pl.semaphore_signal(
            barrier, inc=1, device_id=(row, near_x(k)), device_id_type=pl.DeviceIdType.MESH
        )
    local[0].wait()
    for o in range(n_rows):
        asked_out[o, :, 0:cap] = requests[o : o + 1, :]
    pl.semaphore_wait(barrier, n_rows + n_cols - 2)

    def ask(i, carry):
        d = partner(i)
        remote(asked_out.at[d], asked_in.at[row], asked_sem.at[0], asked_sem.at[1], d, col).start()
        return carry

    lax.fori_loop(0, n_rows - 1, ask, 0)
    asked_in[row] = asked_out[row]

    local[1].wait()
    rows_here = mutants[...].reshape(mutants32.shape)
    gram = fold(rows_here, rows_here)
    share = gram.shape[0] // n_cols
    for q in range(n_cols):
        gram_mine[q] = gram[q * share : (q + 1) * share]
    blocks_here = mutants.shape[0]
    me = row * n_cols + col
    for h in range(hubs):
        block = hub_block_s[h]
        own = mutants[lax.rem(block, blocks_here)]
        owner = jnp.full(own.shape, lax.div(block, blocks_here), jnp.int32)
        hub_mine[h] = jnp.where(owner == me, own.astype(f32), 0.0).astype(bf16)
    per_col = hubs // n_cols
    for k in (2, 1, 3):
        q = near_x(k)
        remote(
            hub_mine.at[pl.ds(q * per_col, per_col)], hub_x.at[col],
            hub_send.at[0], hub_recv.at[0], row, q,
        ).start()
        remote(
            gram_mine.at[q], gram_x.at[col], gram_send.at[0], gram_recv.at[0], row, q
        ).start()
    for o in range(blocks_here):
        mutants32[o * tile : (o + 1) * tile] = mutants[o].astype(f32)

    drain(asked_in.at[pl.ds(0, n_rows - 1)], asked_sem.at[1])
    fetch = pltpu.make_async_copy(asked_in, asked_s, local_sem.at[6])
    fetch.start()
    fetch.wait()

    def gather_for(d):
        for j in range(cap):
            rows32[j : j + 1, :] = mutants32[pl.ds(asked_s[d, 0, j], 1), :]
        return rows32[...].astype(bf16)

    def serve(i, carry):
        d = partner(i)
        answers[i] = gather_for(d)
        remote(
            answers.at[i], received.at[row], answer_send, answer_recv.at[row], d, col
        ).start()
        return carry

    def prepare(n, carry):
        w = weights[n].astype(f32)
        p = pattern[n].astype(f32)
        weights[n] = (w * p).astype(bf16)
        confidence[n] = (p * (1.0 + w)).astype(bf16)
        return carry

    others = n_rows - 1
    cuts = [others * s // 5 for s in range(6)]

    lax.fori_loop(cuts[0], cuts[1], serve, 0)
    drain(hub_x.at[pl.ds(0, n_cols - 1)], hub_recv.at[0])
    drain(gram_x.at[pl.ds(0, n_cols - 1)], gram_recv.at[0])
    piece = hub_xsum.shape[1]
    total = hub_mine[pl.ds(col * per_col, per_col)]
    for k in range(1, n_cols):
        total = total + hub_x[near_x(k)]
    hub_xsum[...] = total.reshape(hub_xsum.shape)
    gsum = gram_mine[col]
    for k in range(1, n_cols):
        gsum = gsum + gram_x[near_x(k)]
    gram_xsum[...] = gsum
    for k in range(1, ring):
        e = near_y(k)
        remote(
            hub_xsum.at[e], hub_y.at[yc], hub_send.at[1], hub_recv.at[1], z * ring + e, col
        ).start()
        remote(
            gram_xsum, gram_y.at[yc], gram_send.at[1], gram_recv.at[1], z * ring + e, col
        ).start()

    lax.fori_loop(cuts[1], cuts[2], serve, 0)
    drain(hub_y.at[pl.ds(0, ring - 1)], hub_recv.at[1])
    drain(gram_y.at[pl.ds(0, ring - 1)], gram_recv.at[1])
    total = hub_xsum[yc]
    gsum = gram_xsum[...]
    for k in range(1, ring):
        total = total + hub_y[near_y(k)]
        gsum = gsum + gram_y[near_y(k)]
    hub_ysum[...] = total
    gram_ysum[...] = gsum
    for k in range(1, planes):
        e = near_z(k)
        remote(
            hub_ysum, hub_z.at[z], hub_send.at[2], hub_recv.at[2], e * ring + yc, col
        ).start()
        remote(
            gram_ysum, gram_z.at[z], gram_send.at[2], gram_recv.at[2], e * ring + yc, col
        ).start()

    lax.fori_loop(cuts[2], cuts[3], serve, 0)
    drain(hub_z.at[pl.ds(0, planes - 1)], hub_recv.at[2])
    drain(gram_z.at[pl.ds(0, planes - 1)], gram_recv.at[2])
    total = hub_ysum[...]
    gsum = gram_ysum[...]
    for k in range(1, planes):
        total = total + hub_z[near_z(k)]
        gsum = gsum + gram_z[near_z(k)]
    pieces = ring // per_col
    my_piece = hub_share.at[lax.div(yc, pieces), lax.rem(yc, pieces)]
    my_piece[...] = total
    gram_zsum[...] = gsum
    for k in range(1, ring):
        e = near_y(k)
        remote(
            my_piece, my_piece, hub_send.at[3], hub_recv.at[3], z * ring + e, col
        ).start()
    for k in range(1, n_cols):
        remote(
            gram_zsum, gram_all.at[col], gram_send.at[3], gram_recv.at[3], row, near_x(k)
        ).start()
    gram_all[col] = gsum

    lax.fori_loop(cuts[3], cuts[4], serve, 0)
    drain(hub_y.at[pl.ds(0, ring - 1)], hub_recv.at[3])
    my_hubs = pl.ds(col * per_col, per_col)
    for k in range(1, n_cols):
        remote(
            hub_share, hub_all.at[my_hubs], hub_send.at[4], hub_recv.at[4], row, near_x(k)
        ).start()
    lax.fori_loop(cuts[4], cuts[5], serve, 0)
    received[row] = gather_for(row)
    hub_all[my_hubs] = hub_share[...]
    local[4].wait()
    local[5].wait()
    lax.fori_loop(0, tiles, prepare, 0)
    local[3].wait()
    quarter = start.shape[0] // n_cols
    block_quarters = tile // quarter
    for q in range(n_cols):
        start_half[q // block_quarters, q % block_quarters] = start[q * quarter : (q + 1) * quarter].astype(bf16)
    drain(hub_all.at[pl.ds(0, hubs - per_col)], hub_recv.at[4])
    drain(gram_all.at[pl.ds(0, n_cols - 1)], gram_recv.at[3])


    def hub_tile(n):
        part = hub_all[hub_pick_s[n]]
        return part.reshape(tile, part.shape[-1])

    def add_up(step, block, product):
        parts = product.reshape(block_quarters, quarter, product.shape[-1])
        covers = jnp.full(parts.shape, block, jnp.int32)
        for b in range(2):
            at = slice(b * block_quarters, (b + 1) * block_quarters)
            terms[step, at] += jnp.where(covers == b, parts, 0.0)

    def scores_of(vector, n, factors):
        b = block_s[n]
        v = vector[b].reshape(tile, factors.shape[-1])
        weighted = (across(v, factors) * weights[n].astype(f32)).astype(bf16)
        return b, weighted

    def first(n, factors):
        b, weighted = scores_of(start_half, n, factors)
        add_up(0, b, plain(confidence[n], factors) - plain(weighted, factors))

    def later(step, n, factors):
        b, weighted = scores_of(direction_half.at[step - 1], n, factors)
        add_up(step, b, plain(weighted, factors))

    for step in range(ITERS + 1):
        terms[step] = jnp.zeros(terms.shape[1:], f32)

    def hub_first(n, carry):
        first(n, hub_tile(n))
        return carry

    lax.fori_loop(0, hub_tiles, hub_first, 0)

    def arrive(i, carry):
        o = partner(i)
        remote(
            answers.at[i], received.at[o], answer_send, answer_recv.at[o], o, col
        ).wait_recv()
        tail32[pl.ds(pl.multiple_of(o * cap, cap), cap), :] = received[o].astype(f32)
        return carry

    lax.fori_loop(0, others, arrive, 0)
    tail32[pl.ds(pl.multiple_of(row * cap, cap), cap), :] = received[row].astype(f32)

    def tail_first(l, carry):
        for i in range(tile):
            tile32[i : i + 1, :] = tail32[pl.ds(pick_s[l * tile + i], 1), :]
        factors = tile32[...].astype(bf16)
        tail[l] = factors
        first(l + hub_tiles, factors)
        return carry

    local[2].wait()
    lax.fori_loop(0, tail_tiles, tail_first, 0)

    def reduce_terms(step):
        for k in (2, 1, 3):
            q = near_x(k)
            remote(
                terms.at[step, q], terms_in.at[step, col],
                terms_send.at[step], terms_recv.at[step], row, q,
            ).start()
        drain(terms_in.at[step, pl.ds(0, n_cols - 1)], terms_recv.at[step])
        total = terms[step, col]
        for k in range(1, n_cols):
            total = total + terms_in[step, near_x(k)]
        return total

    gram_matrix = gram_all[...].reshape(gram.shape)

    def operator_rest(vector):
        return (
            jnp.dot(vector, gram_matrix, precision=highest, preferred_element_type=f32)
            + ridge * vector
        )

    solution = start[pl.ds(pl.multiple_of(col * quarter, quarter), quarter), :]
    residual = reduce_terms(0) - operator_rest(solution)
    direction = residual
    norm_now = jnp.sum(residual * residual, axis=1, keepdims=True)
    for iteration in range(ITERS):
        mine = direction_half.at[
            iteration, lax.div(col, block_quarters), lax.rem(col, block_quarters)
        ]
        mine[...] = direction.astype(bf16)
        for k in (2, 1, 3):
            remote(
                mine, mine, dir_send.at[iteration], dir_recv.at[iteration], row, near_x(k)
            ).start()
        rest = operator_rest(direction)
        drain(hub_xsum.at[pl.ds(0, dir_words)], dir_recv.at[iteration])

        def hub_later(n, carry):
            later(iteration + 1, n, hub_tile(n))
            return carry

        def tail_later(l, carry):
            later(iteration + 1, l + hub_tiles, tail[l])
            return carry

        lax.fori_loop(0, hub_tiles, hub_later, 0)
        lax.fori_loop(0, tail_tiles, tail_later, 0)
        applied = reduce_terms(iteration + 1) + rest
        step_size = norm_now / (jnp.sum(direction * applied, axis=1, keepdims=True) + tiny)
        solution = solution + step_size * direction
        residual = residual - step_size * applied
        norm_next = jnp.sum(residual * residual, axis=1, keepdims=True)
        direction = residual + norm_next / (norm_now + tiny) * direction
        norm_now = norm_next
    solution_ref[...] = solution
    residual_ref[...] = residual

    drain(asked_out.at[pl.ds(0, n_rows - 1)], asked_sem.at[0])
    drain(answers.at[pl.ds(0, n_rows - 1)], answer_send)
    drain(hub_x.at[pl.ds(0, n_cols - 1)], hub_send.at[0])
    drain(hub_y.at[pl.ds(0, ring - 1)], hub_send.at[1])
    drain(hub_z.at[pl.ds(0, planes - 1)], hub_send.at[2])
    drain(hub_y.at[pl.ds(0, ring - 1)], hub_send.at[3])
    drain(hub_all.at[pl.ds(0, hubs - per_col)], hub_send.at[4])
    drain(gram_x.at[pl.ds(0, n_cols - 1)], gram_send.at[0])
    drain(gram_y.at[pl.ds(0, ring - 1)], gram_send.at[1])
    drain(gram_z.at[pl.ds(0, planes - 1)], gram_send.at[2])
    drain(gram_all.at[pl.ds(0, n_cols - 1)], gram_send.at[3])
    for step in range(ITERS + 1):
        drain(terms_in.at[step, pl.ds(0, n_cols - 1)], terms_send.at[step])
    for iteration in range(ITERS):
        drain(hub_xsum.at[pl.ds(0, dir_words)], dir_send.at[iteration])


def per_device(
    n_rows,
    n_cols,
    mutant_factors,
    test_factors,
    weights,
    pattern,
    tile_block,
    hub_pick,
    hub_blocks,
    tail_req,
    tail_pick,
):
    mutant_rows, width = mutant_factors.shape
    tile = weights.shape[-1]
    tiles = weights.shape[2]
    hub_tiles = hub_pick.shape[2]
    hubs = hub_blocks.shape[0]
    cap = tail_req.shape[-1]
    full_rows = test_factors.shape[0]
    share = full_rows // n_cols
    slots = (tiles - hub_tiles) * tile
    ring = 8 if n_rows % 64 == 0 else 2
    planes = n_rows // ring
    per_col = hubs // n_cols
    piece = per_col * tile // ring
    gram_share = width // n_cols
    dims = (n_rows, n_cols, planes, ring, cap, tile, tiles, hub_tiles, hubs)
    vmem = pltpu.VMEM
    dma = pltpu.SemaphoreType.DMA
    scratch = [
        vmem((mutant_rows // tile, tile, width), bf16),
        vmem((mutant_rows, width), f32),
        vmem((full_rows, width), f32),
        vmem((tiles, tile, tile), bf16),
        vmem((tiles, tile, tile), jnp.int32),
        vmem((tiles, tile, tile), bf16),
        vmem((n_rows, cap), jnp.int32),
        pltpu.SMEM((slots,), jnp.int32),
        vmem((n_rows, 1, 128), jnp.int32),
        vmem((n_rows, 1, 128), jnp.int32),
        pltpu.SMEM((n_rows, 1, 128), jnp.int32),
        vmem((cap, width), f32),
        vmem((n_rows, cap, width), bf16),
        vmem((n_rows, cap, width), bf16),
        vmem((slots, width), f32),
        vmem((tile, width), f32),
        vmem((tiles - hub_tiles, tile, width), bf16),
        vmem((hubs, tile, width), bf16),
        vmem((n_cols, per_col, tile, width), bf16),
        vmem((ring, piece, width), bf16),
        vmem((ring, piece, width), bf16),
        vmem((piece, width), bf16),
        vmem((planes, piece, width), bf16),
        vmem((per_col, ring // per_col, piece, width), bf16),
        vmem((hubs, ring // per_col, piece, width), bf16),
        vmem((n_cols, gram_share, width), f32),
        vmem((n_cols, gram_share, width), f32),
        vmem((gram_share, width), f32),
        vmem((ring, gram_share, width), f32),
        vmem((gram_share, width), f32),
        vmem((planes, gram_share, width), f32),
        vmem((gram_share, width), f32),
        vmem((n_cols, gram_share, width), f32),
        vmem((2, n_cols // 2, share, width), bf16),
        vmem((ITERS, 2, n_cols // 2, share, width), bf16),
        vmem((ITERS + 1, n_cols, share, width), f32),
        vmem((ITERS + 1, n_cols, share, width), f32),
        dma((7,)),
        dma((2,)),
        dma,
        dma((n_rows,)),
        dma((5,)),
        dma((5,)),
        dma((4,)),
        dma((4,)),
        dma((ITERS + 1,)),
        dma((ITERS + 1,)),
        dma((ITERS,)),
        dma((ITERS,)),
    ]
    anywhere = pl.BlockSpec(memory_space=pl.ANY)
    scalars = pl.BlockSpec(memory_space=pltpu.SMEM)
    out = jax.ShapeDtypeStruct((share, width), f32)
    return pl.pallas_call(
        functools.partial(kernel, dims),
        out_shape=(out, out),
        in_specs=[anywhere] * 6 + [scalars] * 3,
        out_specs=(pl.BlockSpec(memory_space=vmem),) * 2,
        scratch_shapes=scratch,
        compiler_params=pltpu.CompilerParams(
            collective_id=0, has_side_effects=True, vmem_limit_bytes=56 * 1024 * 1024
        ),
    )(
        mutant_factors.reshape(-1, tile, width),
        test_factors,
        weights.reshape(weights.shape[2:]),
        pattern.reshape(pattern.shape[2:]),
        tail_req.reshape(tail_req.shape[2:]),
        tail_pick.reshape(slots),
        tile_block.reshape(tiles),
        hub_pick.reshape(hub_tiles),
        hub_blocks,
    )


def solution(mesh):
    in_specs = (
        P(("rows", "cols"), None),
        P("rows", None),
        P("rows", "cols", None, None, None),
        P("rows", "cols", None, None, None),
        P("rows", "cols", None),
        P("rows", "cols", None),
        P(),
        P("rows", "cols", None, None),
        P("rows", "cols", None),
    )
    out_specs = (P(("rows", "cols"), None), P(("rows", "cols"), None))
    return jax.shard_map(
        functools.partial(per_device, mesh.shape["rows"], mesh.shape["cols"]),
        mesh=mesh,
        in_specs=in_specs,
        out_specs=out_specs,
        check_vma=False,
    )
```

time: 737 us -> 119 us (0.16)
  waiting for transfers between devices: 558 us -> 0 us
  Pallas kernels: 0 us -> 115 us
  matrix products: 56.3 us -> 0 us
  local copies, waits for them, and re-layouts: 56.8 us -> 2.95 us
  between operations: 34.1 us -> 0.64 us
  starting transfers between devices: 18.2 us -> 0 us
  other arithmetic: 13 us -> 0 us
    psum x5 -> x0, waiting for transfers between devices: 551 us -> none  [the longest x1 213 us: from_root(): return lax.psum(jnp.where(mine, shard, jnp.zeros_like(shard)), axis)]
    pallas_call x0 -> x1, Pallas kernels: none -> 115 us  [per_device(): pl.pallas_call(functools.partial(kernel, dims), out_shape=(out, out), in_...]
    dot_general x16 -> x0, matrix products: 56.3 us -> none  [the longest x3 20.5 us: tile_terms(): jnp.einsum('ntm,nmk->ntk', weighted, tile_factors, preferred_element_type...]
    gather x2 -> x0, local copies, waits for them, and re-layouts: 30.2 us -> none  [the longest x1 15.1 us: per_device(): jnp.take(mutant_factors, lax.all_to_all(requests, 'rows', split_axis=0, c...]
    all_to_all x2 -> x0, starting transfers between devices: 17.8 us -> none  [the longest x1 12.1 us: per_device(): lax.all_to_all(requests, 'rows', split_axis=0, concat_axis=0, tiled=True)]
    dot_general x2 -> x0, local copies, waits for them, and re-layouts: 11 us -> none  [tile_terms(): jnp.einsum('ntm,nmk->ntk', weighted, tile_factors, preferred_element_type...]
    another operation x9 -> x0, local copies, waits for them, and re-layouts: 8.98 us -> none  [per_device(): hub_rows = jnp.stack(fetched)]
  transfers between devices with their start and end apart: 7 -> 0, of which waited for: 6 -> 0; matrix products, arithmetic and copies ran while one was open for 10% -> 0% of each run, Pallas kernels for 0% -> 0%
where the time goes in v1:
time: 119 us
  Pallas kernels  115 us (97%)
  local copies, waits for them, and re-layouts  2.95 us (2%)
    pallas_call x1, Pallas kernels, per_device(): pl.pallas_call(functools.partial(kernel, dims), out_shape=(out, out), in_...  115 us
    unnamed x2, local copies, waits for them, and re-layouts  2.95 us

profile of v1, /device:TPU:8, one launch (start us, length us, event | category | flops | bytes accessed | tf_op | source)
XLA Modules:
  0.0 119.0 jit_solution(7044575502011584102)
XLA Ops:
  0.6 115.5 %shard_map.104 = (f32[128,128]{1,0:T(8,128)}, f32[128,128]{1,0:T(8,128)}) custom-call(bf16[8,256,128]{2,1,0:T(8,128)(2,1)} %bitcast.9, f32[512,128]{1,0:T(8,128)} %start_h.1, bf16[28,256,256]{2,1,0:T(8,128)(2,1)} %bitcast.8, s32[28,256,256]{2,1,0:T(8,128)} %bitcast.7, s32[64,80]{1,0:T(8,128)} %bitcast.10, s32[5120]{0:T(1024)} %bitcast.11, s32[28]{0:T(128)} %bitcast.12, ...), custom_call_target="tpu_custom_call" | custom-call | tf_op jit(solution)/shard_map/pallas_call | solution.py:524
  116.1 1.5 %copy.13 = f32[128,128]{1,0:T(8,128)} copy(f32[128,128]{1,0:T(8,128)} %get-tuple-element.4) | data formatting | bytes 131072
  117.6 1.5 %copy.14 = f32[128,128]{1,0:T(8,128)} copy(f32[128,128]{1,0:T(8,128)} %get-tuple-element.5) | data formatting | bytes 131072

commit v2 on v1

--- a/solution.py
+++ b/solution.py
@@ -8,6 +8,7 @@
 from jax.sharding import PartitionSpec as P
 
 ITERS = 2
+GROUP = 4
 
 ridge = 0.1
 tiny = 1e-06
@@ -54,8 +55,7 @@
     block_s,
     hub_pick_s,
     hub_block_s,
-    solution_ref,
-    residual_ref,
+    out_ref,
     mutants,
     mutants32,
     start,
@@ -72,7 +72,7 @@
     received,
     tail32,
     tile32,
-    tail,
+    factors,
     hub_mine,
     hub_x,
     hub_xsum,
@@ -87,7 +87,6 @@
     gram_y,
     gram_ysum,
     gram_z,
-    gram_zsum,
     gram_all,
     start_half,
     direction_half,
@@ -169,30 +168,31 @@
     asked_in[row] = asked_out[row]
 
     local[1].wait()
-    rows_here = mutants[...].reshape(mutants32.shape)
-    gram = fold(rows_here, rows_here)
-    share = gram.shape[0] // n_cols
-    for q in range(n_cols):
-        gram_mine[q] = gram[q * share : (q + 1) * share]
     blocks_here = mutants.shape[0]
+    for o in range(blocks_here):
+        mutants32[o * tile : (o + 1) * tile] = mutants[o].astype(f32)
     me = row * n_cols + col
+    per_col = hubs // n_cols
+    pieces = ring // per_col
     for h in range(hubs):
         block = hub_block_s[h]
         own = mutants[lax.rem(block, blocks_here)]
         owner = jnp.full(own.shape, lax.div(block, blocks_here), jnp.int32)
-        hub_mine[h] = jnp.where(owner == me, own.astype(f32), 0.0).astype(bf16)
-    per_col = hubs // n_cols
-    for k in (2, 1, 3):
-        q = near_x(k)
-        remote(
-            hub_mine.at[pl.ds(q * per_col, per_col)], hub_x.at[col],
-            hub_send.at[0], hub_recv.at[0], row, q,
-        ).start()
-        remote(
-            gram_mine.at[q], gram_x.at[col], gram_send.at[0], gram_recv.at[0], row, q
-        ).start()
-    for o in range(blocks_here):
-        mutants32[o * tile : (o + 1) * tile] = mutants[o].astype(f32)
+        kept = jnp.where(owner == me, own.astype(f32), 0.0).astype(bf16)
+        at = slice(h % per_col * pieces, (h % per_col + 1) * pieces)
+        hub_mine[h // per_col, at] = kept.reshape(pieces, tile // pieces, kept.shape[-1])
+
+    def send_hub_x(p):
+        q = near_x(lax.rem(p, n_cols - 1) + 1)
+        e = lax.div(p, n_cols - 1)
+        remote(
+            hub_mine.at[q, e], hub_x.at[col, e], hub_send.at[0], hub_recv.at[0], row, q
+        ).start()
+
+    hub_pieces = (n_cols - 1) * ring
+    early = hub_pieces // 3
+    for p in range(early):
+        send_hub_x(p)
 
     drain(asked_in.at[pl.ds(0, n_rows - 1)], asked_sem.at[1])
     fetch = pltpu.make_async_copy(asked_in, asked_s, local_sem.at[6])
@@ -220,126 +220,121 @@
         return carry
 
     others = n_rows - 1
-    cuts = [others * s // 5 for s in range(6)]
-
+    def serve_and_send(i, carry):
+        serve(i, carry)
+        send_hub_x(early + i)
+        return carry
+
+    def serve_and_send(i, carry):
+        serve(i, carry)
+        send_hub_x(early + i)
+        return carry
+
+    cuts = [hub_pieces - early, others * 4 // 9, others * 2 // 3]
+    ready = [tiles * c // 4 for c in range(5)]
+
+    first_cut = hub_pieces - early
+    cuts = [first_cut] + [first_cut + (others - first_cut) * c // 47 for c in (12, 26)]
+    ready = [tiles * c // 3 for c in range(4)]
+
+    lax.fori_loop(0, cuts[0], serve_and_send, 0)
+    rows_here = mutants[...].reshape(mutants32.shape)
+    gram = fold(rows_here, rows_here)
+    share = gram_mine.shape[1]
+    for q in range(ring):
+        gram_mine[q] = gram[q * share : (q + 1) * share]
+    for k in range(1, ring):
+        e = near_y(k)
+        remote(
+            gram_mine.at[e], gram_y.at[yc], gram_send.at[0], gram_recv.at[0], z * ring + e, col
+        ).start()
     lax.fori_loop(cuts[0], cuts[1], serve, 0)
+    local[4].wait()
+    local[5].wait()
+    lax.fori_loop(ready[0], ready[1], prepare, 0)
+
     drain(hub_x.at[pl.ds(0, n_cols - 1)], hub_recv.at[0])
-    drain(gram_x.at[pl.ds(0, n_cols - 1)], gram_recv.at[0])
-    piece = hub_xsum.shape[1]
-    total = hub_mine[pl.ds(col * per_col, per_col)]
+    total = hub_mine[col]
     for k in range(1, n_cols):
         total = total + hub_x[near_x(k)]
-    hub_xsum[...] = total.reshape(hub_xsum.shape)
-    gsum = gram_mine[col]
+    hub_xsum[...] = total
+    for k in range(1, ring):
+        e = near_y(k)
+        remote(
+            hub_xsum.at[e], hub_y.at[yc], hub_send.at[1], hub_recv.at[1], z * ring + e, col
+        ).start()
+    drain(gram_y.at[pl.ds(0, ring - 1)], gram_recv.at[0])
+    gsum = gram_mine[yc]
+    for k in range(1, ring):
+        gsum = gsum + gram_y[near_y(k)]
+    gram_ysum[...] = gsum
+    for k in range(1, n_cols):
+        remote(
+            gram_ysum, gram_x.at[col], gram_send.at[1], gram_recv.at[1], row, near_x(k)
+        ).start()
+    lax.fori_loop(cuts[1], cuts[2], serve, 0)
+    lax.fori_loop(ready[1], ready[2], prepare, 0)
+
+    drain(hub_y.at[pl.ds(0, ring - 1)], hub_recv.at[1])
+    total = hub_xsum[yc]
+    for k in range(1, ring):
+        total = total + hub_y[near_y(k)]
+    hub_ysum[...] = total
+    for k in range(1, planes):
+        e = near_z(k)
+        remote(
+            hub_ysum, hub_z.at[z], hub_send.at[2], hub_recv.at[2], e * ring + yc, col
+        ).start()
+    drain(gram_x.at[pl.ds(0, n_cols - 1)], gram_recv.at[1])
+    gsum = gram_ysum[...]
     for k in range(1, n_cols):
         gsum = gsum + gram_x[near_x(k)]
     gram_xsum[...] = gsum
-    for k in range(1, ring):
-        e = near_y(k)
-        remote(
-            hub_xsum.at[e], hub_y.at[yc], hub_send.at[1], hub_recv.at[1], z * ring + e, col
-        ).start()
-        remote(
-            gram_xsum, gram_y.at[yc], gram_send.at[1], gram_recv.at[1], z * ring + e, col
-        ).start()
-
-    lax.fori_loop(cuts[1], cuts[2], serve, 0)
-    drain(hub_y.at[pl.ds(0, ring - 1)], hub_recv.at[1])
-    drain(gram_y.at[pl.ds(0, ring - 1)], gram_recv.at[1])
-    total = hub_xsum[yc]
-    gsum = gram_xsum[...]
-    for k in range(1, ring):
-        total = total + hub_y[near_y(k)]
-        gsum = gsum + gram_y[near_y(k)]
-    hub_ysum[...] = total
-    gram_ysum[...] = gsum
+    lax.fori_loop(cuts[2], others, serve, 0)
     for k in range(1, planes):
         e = near_z(k)
         remote(
-            hub_ysum, hub_z.at[z], hub_send.at[2], hub_recv.at[2], e * ring + yc, col
-        ).start()
-        remote(
-            gram_ysum, gram_z.at[z], gram_send.at[2], gram_recv.at[2], e * ring + yc, col
-        ).start()
-
-    lax.fori_loop(cuts[2], cuts[3], serve, 0)
-    drain(hub_z.at[pl.ds(0, planes - 1)], hub_recv.at[2])
-    drain(gram_z.at[pl.ds(0, planes - 1)], gram_recv.at[2])
-    total = hub_ysum[...]
-    gsum = gram_ysum[...]
-    for k in range(1, planes):
-        total = total + hub_z[near_z(k)]
-        gsum = gsum + gram_z[near_z(k)]
-    pieces = ring // per_col
-    my_piece = hub_share.at[lax.div(yc, pieces), lax.rem(yc, pieces)]
-    my_piece[...] = total
-    gram_zsum[...] = gsum
-    for k in range(1, ring):
-        e = near_y(k)
-        remote(
-            my_piece, my_piece, hub_send.at[3], hub_recv.at[3], z * ring + e, col
-        ).start()
-    for k in range(1, n_cols):
-        remote(
-            gram_zsum, gram_all.at[col], gram_send.at[3], gram_recv.at[3], row, near_x(k)
-        ).start()
-    gram_all[col] = gsum
-
-    lax.fori_loop(cuts[3], cuts[4], serve, 0)
-    drain(hub_y.at[pl.ds(0, ring - 1)], hub_recv.at[3])
-    my_hubs = pl.ds(col * per_col, per_col)
-    for k in range(1, n_cols):
-        remote(
-            hub_share, hub_all.at[my_hubs], hub_send.at[4], hub_recv.at[4], row, near_x(k)
-        ).start()
-    lax.fori_loop(cuts[4], cuts[5], serve, 0)
+            gram_xsum, gram_z.at[z], gram_send.at[2], gram_recv.at[2], e * ring + yc, col
+        ).start()
+    lax.fori_loop(ready[2], ready[3], prepare, 0)
     received[row] = gather_for(row)
-    hub_all[my_hubs] = hub_share[...]
-    local[4].wait()
-    local[5].wait()
-    lax.fori_loop(0, tiles, prepare, 0)
     local[3].wait()
     quarter = start.shape[0] // n_cols
     block_quarters = tile // quarter
     for q in range(n_cols):
-        start_half[q // block_quarters, q % block_quarters] = start[q * quarter : (q + 1) * quarter].astype(bf16)
-    drain(hub_all.at[pl.ds(0, hubs - per_col)], hub_recv.at[4])
-    drain(gram_all.at[pl.ds(0, n_cols - 1)], gram_recv.at[3])
-
-
-    def hub_tile(n):
-        part = hub_all[hub_pick_s[n]]
-        return part.reshape(tile, part.shape[-1])
-
-    def add_up(step, block, product):
-        parts = product.reshape(block_quarters, quarter, product.shape[-1])
-        covers = jnp.full(parts.shape, block, jnp.int32)
-        for b in range(2):
-            at = slice(b * block_quarters, (b + 1) * block_quarters)
-            terms[step, at] += jnp.where(covers == b, parts, 0.0)
-
-    def scores_of(vector, n, factors):
-        b = block_s[n]
-        v = vector[b].reshape(tile, factors.shape[-1])
-        weighted = (across(v, factors) * weights[n].astype(f32)).astype(bf16)
-        return b, weighted
-
-    def first(n, factors):
-        b, weighted = scores_of(start_half, n, factors)
-        add_up(0, b, plain(confidence[n], factors) - plain(weighted, factors))
-
-    def later(step, n, factors):
-        b, weighted = scores_of(direction_half.at[step - 1], n, factors)
-        add_up(step, b, plain(weighted, factors))
-
+        start_half[q // block_quarters, q % block_quarters] = start[
+            q * quarter : (q + 1) * quarter
+        ].astype(bf16)
     for step in range(ITERS + 1):
         terms[step] = jnp.zeros(terms.shape[1:], f32)
 
-    def hub_first(n, carry):
-        first(n, hub_tile(n))
-        return carry
-
-    lax.fori_loop(0, hub_tiles, hub_first, 0)
+    def group(step, vector, base):
+        parts = []
+        for u in range(GROUP):
+            n = base + u
+            b = block_s[n]
+            v = vector[b].reshape(tile, factors.shape[-1])
+            scores = across(v, factors[n])
+            parts.append((n, b, (scores * weights[n].astype(f32)).astype(bf16)))
+        sums = [None, None]
+        for n, b, weighted in parts:
+            product = plain(weighted, factors[n])
+            if step == 0:
+                product = plain(confidence[n], factors[n]) - product
+            covers = jnp.full(product.shape, b, jnp.int32)
+            for half in range(2):
+                kept = jnp.where(covers == half, product, 0.0)
+                sums[half] = kept if sums[half] is None else sums[half] + kept
+        for half in range(2):
+            at = slice(half * block_quarters, (half + 1) * block_quarters)
+            terms[step, at] += sums[half].reshape(block_quarters, quarter, factors.shape[-1])
+
+    def groups(step, vector, first, last):
+        def one(g, carry):
+            group(step, vector, g * GROUP)
+            return carry
+
+        lax.fori_loop(first // GROUP, last // GROUP, one, 0)
 
     def arrive(i, carry):
         o = partner(i)
@@ -349,19 +344,71 @@
         tail32[pl.ds(pl.multiple_of(o * cap, cap), cap), :] = received[o].astype(f32)
         return carry
 
-    lax.fori_loop(0, others, arrive, 0)
+    lax.fori_loop(0, cuts[2], arrive, 0)
+
+    drain(hub_z.at[pl.ds(0, planes - 1)], hub_recv.at[2])
+    total = hub_ysum[...]
+    for k in range(1, planes):
+        total = total + hub_z[near_z(k)]
+    core = lax.rem(yc, 2)
+    my_piece = hub_share.at[lax.div(yc, pieces), lax.div(lax.rem(yc, pieces), 2)]
+    my_piece[...] = total
+    for k in range(2, ring, 2):
+        remote(
+            my_piece, my_piece, hub_send.at[3], hub_recv.at[3], z * ring + near_y(k), col
+        ).start()
+    lax.fori_loop(cuts[2], others, arrive, 0)
     tail32[pl.ds(pl.multiple_of(row * cap, cap), cap), :] = received[row].astype(f32)
 
-    def tail_first(l, carry):
+    def tail_tile(l, carry):
         for i in range(tile):
             tile32[i : i + 1, :] = tail32[pl.ds(pick_s[l * tile + i], 1), :]
-        factors = tile32[...].astype(bf16)
-        tail[l] = factors
-        first(l + hub_tiles, factors)
+        factors[l + hub_tiles] = tile32[...].astype(bf16)
         return carry
 
     local[2].wait()
-    lax.fori_loop(0, tail_tiles, tail_first, 0)
+
+    drain(hub_y.at[pl.ds(0, ring // 2 - 1)], hub_recv.at[3])
+    halves = pieces // 2
+    for h in range(per_col):
+        at = col * per_col + h
+        for k in (2, 1, 3):
+            remote(
+                hub_share.at[h], hub_all.at[at, core],
+                hub_send.at[4], hub_recv.at[4], row, near_x(k),
+            ).start()
+        hub_all[at, core] = hub_share[h]
+
+    drain(gram_z.at[pl.ds(0, planes - 1)], gram_recv.at[2])
+    gsum = gram_xsum[...]
+    for k in range(1, planes):
+        gsum = gsum + gram_z[near_z(k)]
+    gram_all[yc] = gsum
+    for k in range(1, ring):
+        remote(
+            gram_all.at[yc], gram_all.at[yc], gram_send.at[3], gram_recv.at[3],
+            z * ring + near_y(k), col,
+        ).start()
+    middle = tail_tiles * 3 // 4
+    lax.fori_loop(0, middle, tail_tile, 0)
+
+    drain(hub_x.at[pl.ds(0, n_cols - 1), pl.ds(0, per_col * halves)], hub_recv.at[4])
+    sibling = row + 1 - 2 * core
+    for h in range(hubs):
+        remote(
+            hub_all.at[h, core], hub_all.at[h, core],
+            hub_send.at[5], hub_recv.at[5], sibling, col,
+        ).start()
+    lax.fori_loop(middle, tail_tiles, tail_tile, 0)
+    groups(0, start_half, hub_tiles, tiles)
+    drain(hub_mine.at[pl.ds(0, n_cols // 2)], hub_recv.at[5])
+    for n in range(hub_tiles):
+        part = hub_all[hub_pick_s[n]]
+        for m in range(halves):
+            for c in range(2):
+                at = (2 * m + c) * part.shape[2]
+                factors[n, at : at + part.shape[2]] = part[c, m]
+    groups(0, start_half, 0, hub_tiles)
 
     def reduce_terms(step):
         for k in (2, 1, 3):
@@ -376,6 +423,7 @@
             total = total + terms_in[step, near_x(k)]
         return total
 
+    drain(gram_all.at[pl.ds(0, ring - 1)], gram_recv.at[3])
     gram_matrix = gram_all[...].reshape(gram.shape)
 
     def operator_rest(vector):
@@ -400,16 +448,7 @@
         rest = operator_rest(direction)
         drain(hub_xsum.at[pl.ds(0, dir_words)], dir_recv.at[iteration])
 
-        def hub_later(n, carry):
-            later(iteration + 1, n, hub_tile(n))
-            return carry
-
-        def tail_later(l, carry):
-            later(iteration + 1, l + hub_tiles, tail[l])
-            return carry
-
-        lax.fori_loop(0, hub_tiles, hub_later, 0)
-        lax.fori_loop(0, tail_tiles, tail_later, 0)
+        groups(iteration + 1, direction_half.at[iteration], 0, tiles)
         applied = reduce_terms(iteration + 1) + rest
         step_size = norm_now / (jnp.sum(direction * applied, axis=1, keepdims=True) + tiny)
         solution = solution + step_size * direction
@@ -417,20 +456,21 @@
         norm_next = jnp.sum(residual * residual, axis=1, keepdims=True)
         direction = residual + norm_next / (norm_now + tiny) * direction
         norm_now = norm_next
-    solution_ref[...] = solution
-    residual_ref[...] = residual
+    out_ref[0] = solution
+    out_ref[1] = residual
 
     drain(asked_out.at[pl.ds(0, n_rows - 1)], asked_sem.at[0])
     drain(answers.at[pl.ds(0, n_rows - 1)], answer_send)
     drain(hub_x.at[pl.ds(0, n_cols - 1)], hub_send.at[0])
     drain(hub_y.at[pl.ds(0, ring - 1)], hub_send.at[1])
     drain(hub_z.at[pl.ds(0, planes - 1)], hub_send.at[2])
-    drain(hub_y.at[pl.ds(0, ring - 1)], hub_send.at[3])
-    drain(hub_all.at[pl.ds(0, hubs - per_col)], hub_send.at[4])
-    drain(gram_x.at[pl.ds(0, n_cols - 1)], gram_send.at[0])
-    drain(gram_y.at[pl.ds(0, ring - 1)], gram_send.at[1])
+    drain(hub_y.at[pl.ds(0, ring // 2 - 1)], hub_send.at[3])
+    drain(hub_x.at[pl.ds(0, n_cols - 1), pl.ds(0, per_col * halves)], hub_send.at[4])
+    drain(hub_mine.at[pl.ds(0, n_cols // 2)], hub_send.at[5])
+    drain(gram_y.at[pl.ds(0, ring - 1)], gram_send.at[0])
+    drain(gram_x.at[pl.ds(0, n_cols - 1)], gram_send.at[1])
     drain(gram_z.at[pl.ds(0, planes - 1)], gram_send.at[2])
-    drain(gram_all.at[pl.ds(0, n_cols - 1)], gram_send.at[3])
+    drain(gram_all.at[pl.ds(0, ring - 1)], gram_send.at[3])
     for step in range(ITERS + 1):
         drain(terms_in.at[step, pl.ds(0, n_cols - 1)], terms_send.at[step])
     for iteration in range(ITERS):
@@ -463,7 +503,7 @@
     planes = n_rows // ring
     per_col = hubs // n_cols
     piece = per_col * tile // ring
-    gram_share = width // n_cols
+    gram_share = width // ring
     dims = (n_rows, n_cols, planes, ring, cap, tile, tiles, hub_tiles, hubs)
     vmem = pltpu.VMEM
     dma = pltpu.SemaphoreType.DMA
@@ -484,23 +524,22 @@
         vmem((n_rows, cap, width), bf16),
         vmem((slots, width), f32),
         vmem((tile, width), f32),
-        vmem((tiles - hub_tiles, tile, width), bf16),
-        vmem((hubs, tile, width), bf16),
-        vmem((n_cols, per_col, tile, width), bf16),
+        vmem((tiles, tile, width), bf16),
+        vmem((n_cols, ring, piece, width), bf16),
+        vmem((n_cols, ring, piece, width), bf16),
         vmem((ring, piece, width), bf16),
         vmem((ring, piece, width), bf16),
         vmem((piece, width), bf16),
         vmem((planes, piece, width), bf16),
-        vmem((per_col, ring // per_col, piece, width), bf16),
-        vmem((hubs, ring // per_col, piece, width), bf16),
-        vmem((n_cols, gram_share, width), f32),
+        vmem((per_col, ring // per_col // 2, piece, width), bf16),
+        vmem((hubs, 2, ring // per_col // 2, piece, width), bf16),
+        vmem((ring, gram_share, width), f32),
         vmem((n_cols, gram_share, width), f32),
         vmem((gram_share, width), f32),
         vmem((ring, gram_share, width), f32),
         vmem((gram_share, width), f32),
         vmem((planes, gram_share, width), f32),
-        vmem((gram_share, width), f32),
-        vmem((n_cols, gram_share, width), f32),
+        vmem((ring, gram_share, width), f32),
         vmem((2, n_cols // 2, share, width), bf16),
         vmem((ITERS, 2, n_cols // 2, share, width), bf16),
         vmem((ITERS + 1, n_cols, share, width), f32),
@@ -509,8 +548,8 @@
         dma((2,)),
         dma,
         dma((n_rows,)),
-        dma((5,)),
-        dma((5,)),
+        dma((6,)),
+        dma((6,)),
         dma((4,)),
         dma((4,)),
         dma((ITERS + 1,)),
@@ -520,12 +559,11 @@
     ]
     anywhere = pl.BlockSpec(memory_space=pl.ANY)
     scalars = pl.BlockSpec(memory_space=pltpu.SMEM)
-    out = jax.ShapeDtypeStruct((share, width), f32)
-    return pl.pallas_call(
+    both = pl.pallas_call(
         functools.partial(kernel, dims),
-        out_shape=(out, out),
+        out_shape=jax.ShapeDtypeStruct((2, share, width), f32),
         in_specs=[anywhere] * 6 + [scalars] * 3,
-        out_specs=(pl.BlockSpec(memory_space=vmem),) * 2,
+        out_specs=pl.BlockSpec(memory_space=vmem),
         scratch_shapes=scratch,
         compiler_params=pltpu.CompilerParams(
             collective_id=0, has_side_effects=True, vmem_limit_bytes=56 * 1024 * 1024
@@ -541,6 +579,7 @@
         hub_pick.reshape(hub_tiles),
         hub_blocks,
     )
+    return both[0], both[1]
 
 
 def solution(mesh):

time: 119 us -> 95.7 us (0.80)
  Pallas kernels: 115 us -> 93.3 us
  local copies, waits for them, and re-layouts: 2.95 us -> 1.53 us
    pallas_call x1, Pallas kernels: 115 us -> 93.3 us  [per_device(): pl.pallas_call(functools.partial(kernel, dims), out_shape=jax.ShapeDtypeS...]
    unnamed x2 -> x0, local copies, waits for them, and re-layouts: 2.95 us -> none
    squeeze x0 -> x1, local copies, waits for them, and re-layouts: none -> 1.53 us  [per_device(): return (both[0], both[1])]
where the time goes in v2:
time: 95.7 us; the launch traced here: 95.5 us
  Pallas kernels  93.3 us (97%)
  local copies, waits for them, and re-layouts  1.53 us (2%)
    pallas_call x1, Pallas kernels, per_device(): pl.pallas_call(functools.partial(kernel, dims), out_shape=jax.ShapeDtypeS...  93.3 us

profile of v2, /device:TPU:8, one launch (start us, length us, event | category | flops | bytes accessed | tf_op | source)
XLA Modules:
  0.0 95.5 jit_solution(15524550599091670359)
XLA Ops:
  0.6 93.3 %shard_map.104 = f32[2,128,128]{2,1,0:T(8,128)} custom-call(bf16[8,256,128]{2,1,0:T(8,128)(2,1)} %bitcast.13, f32[512,128]{1,0:T(8,128)} %start_h.1, bf16[28,256,256]{2,1,0:T(8,128)(2,1)} %bitcast.12, s32[28,256,256]{2,1,0:T(8,128)} %bitcast.11, s32[64,80]{1,0:T(8,128)} %bitcast.14, s32[5120]{0:T(1024)} %bitcast.15, s32[28]{0:T(128)} %bitcast.16, ...), custom_call_target="tpu_custom_call" | custom-call | tf_op jit(solution)/shard_map/pallas_call | solution.py:562
  94.0 1.5 %slice_bitcast_fusion = (f32[128,128]{1,0:T(8,128)}, f32[128,128]{1,0:T(8,128)}) fusion(f32[2,128,128]{2,1,0:T(8,128)} %shard_map.104), kind=kLoop, calls=%fused_computation | loop fusion | bytes 262144 | tf_op jit(solution)/shard_map/squeeze | solution.py:582

commit v3 on v2

--- a/solution.py
+++ b/solution.py
@@ -9,6 +9,7 @@
 
 ITERS = 2
 GROUP = 4
+LATER = 14
 
 ridge = 0.1
 tiny = 1e-06
@@ -308,33 +309,54 @@
     for step in range(ITERS + 1):
         terms[step] = jnp.zeros(terms.shape[1:], f32)
 
-    def group(step, vector, base):
+    slab = quarter // 2
+
+    def group(step, vector, m, base, size):
         parts = []
-        for u in range(GROUP):
+        for u in range(size):
             n = base + u
             b = block_s[n]
-            v = vector[b].reshape(tile, factors.shape[-1])
+            v = vector[b][:, m * slab : (m + 1) * slab].reshape(tile // 2, factors.shape[-1])
             scores = across(v, factors[n])
-            parts.append((n, b, (scores * weights[n].astype(f32)).astype(bf16)))
+            w = jnp.concatenate(
+                [weights[n, q * quarter + m * slab : q * quarter + (m + 1) * slab]
+                 for q in range(block_quarters)]
+            )
+            parts.append((n, b, (scores * w.astype(f32)).astype(bf16)))
         sums = [None, None]
         for n, b, weighted in parts:
             product = plain(weighted, factors[n])
             if step == 0:
-                product = plain(confidence[n], factors[n]) - product
+                c = jnp.concatenate(
+                    [confidence[n, q * quarter + m * slab : q * quarter + (m + 1) * slab]
+                     for q in range(block_quarters)]
+                )
+                product = plain(c, factors[n]) - product
             covers = jnp.full(product.shape, b, jnp.int32)
             for half in range(2):
                 kept = jnp.where(covers == half, product, 0.0)
                 sums[half] = kept if sums[half] is None else sums[half] + kept
         for half in range(2):
-            at = slice(half * block_quarters, (half + 1) * block_quarters)
-            terms[step, at] += sums[half].reshape(block_quarters, quarter, factors.shape[-1])
-
-    def groups(step, vector, first, last):
+            for q in range(block_quarters):
+                terms[step, half * block_quarters + q, m * slab : (m + 1) * slab] += sums[half][
+                    q * slab : (q + 1) * slab
+                ]
+
+    def groups(step, vector, m, first, last, size):
         def one(g, carry):
-            group(step, vector, g * GROUP)
+            group(step, vector, m, g * size, size)
             return carry
 
-        lax.fori_loop(first // GROUP, last // GROUP, one, 0)
+        lax.fori_loop(first // size, last // size, one, 0)
+
+    def send_terms(step, m):
+        at = pl.ds(m * slab, slab)
+        for k in (2, 1, 3):
+            q = near_x(k)
+            remote(
+                terms.at[step, q, at], terms_in.at[step, col, at],
+                terms_send.at[step, m], terms_recv.at[step, m], row, q,
+            ).start()
 
     def arrive(i, carry):
         o = partner(i)
@@ -400,7 +422,7 @@
             hub_send.at[5], hub_recv.at[5], sibling, col,
         ).start()
     lax.fori_loop(middle, tail_tiles, tail_tile, 0)
-    groups(0, start_half, hub_tiles, tiles)
+    groups(0, start_half, 0, hub_tiles, tiles, GROUP)
     drain(hub_mine.at[pl.ds(0, n_cols // 2)], hub_recv.at[5])
     for n in range(hub_tiles):
         part = hub_all[hub_pick_s[n]]
@@ -408,16 +430,16 @@
             for c in range(2):
                 at = (2 * m + c) * part.shape[2]
                 factors[n, at : at + part.shape[2]] = part[c, m]
-    groups(0, start_half, 0, hub_tiles)
+    groups(0, start_half, 0, 0, hub_tiles, 2 * GROUP)
+    send_terms(0, 0)
+    groups(0, start_half, 1, 0, tiles, LATER // 2)
+    send_terms(0, 1)
 
     def reduce_terms(step):
-        for k in (2, 1, 3):
-            q = near_x(k)
-            remote(
-                terms.at[step, q], terms_in.at[step, col],
-                terms_send.at[step], terms_recv.at[step], row, q,
-            ).start()
-        drain(terms_in.at[step, pl.ds(0, n_cols - 1)], terms_recv.at[step])
+        for m in range(2):
+            drain(
+                terms_in.at[step, pl.ds(0, n_cols - 1), pl.ds(0, slab)], terms_recv.at[step, m]
+            )
         total = terms[step, col]
         for k in range(1, n_cols):
             total = total + terms_in[step, near_x(k)]
@@ -448,7 +470,9 @@
         rest = operator_rest(direction)
         drain(hub_xsum.at[pl.ds(0, dir_words)], dir_recv.at[iteration])
 
-        groups(iteration + 1, direction_half.at[iteration], 0, tiles)
+        for m in range(2):
+            groups(iteration + 1, direction_half.at[iteration], m, 0, tiles, LATER)
+            send_terms(iteration + 1, m)
         applied = reduce_terms(iteration + 1) + rest
         step_size = norm_now / (jnp.sum(direction * applied, axis=1, keepdims=True) + tiny)
         solution = solution + step_size * direction
@@ -472,7 +496,10 @@
     drain(gram_z.at[pl.ds(0, planes - 1)], gram_send.at[2])
     drain(gram_all.at[pl.ds(0, ring - 1)], gram_send.at[3])
     for step in range(ITERS + 1):
-        drain(terms_in.at[step, pl.ds(0, n_cols - 1)], terms_send.at[step])
+        for m in range(2):
+            drain(
+                terms_in.at[step, pl.ds(0, n_cols - 1), pl.ds(0, slab)], terms_send.at[step, m]
+            )
     for iteration in range(ITERS):
         drain(hub_xsum.at[pl.ds(0, dir_words)], dir_send.at[iteration])
 
@@ -552,8 +579,8 @@
         dma((6,)),
         dma((4,)),
         dma((4,)),
-        dma((ITERS + 1,)),
-        dma((ITERS + 1,)),
+        dma((ITERS + 1, 2)),
+        dma((ITERS + 1, 2)),
         dma((ITERS,)),
         dma((ITERS,)),
     ]

time: 95.7 us -> 93.4 us (0.976)
  Pallas kernels: 93.3 us -> 90.9 us
    pallas_call x1, Pallas kernels: 93.3 us -> 90.9 us  [per_device(): pl.pallas_call(functools.partial(kernel, dims), out_shape=jax.ShapeDtypeS...]
where the time goes in v3:
time: 93.4 us; the launch traced here: 93.1 us
  Pallas kernels  90.9 us (97%)
  local copies, waits for them, and re-layouts  1.53 us (2%)
    pallas_call x1, Pallas kernels, per_device(): pl.pallas_call(functools.partial(kernel, dims), out_shape=jax.ShapeDtypeS...  90.9 us

profile of v3, /device:TPU:8, one launch (start us, length us, event | category | flops | bytes accessed | tf_op | source)
XLA Modules:
  0.0 93.1 jit_solution(8414282397746360294)
XLA Ops:
  0.6 90.9 %shard_map.104 = f32[2,128,128]{2,1,0:T(8,128)} custom-call(bf16[8,256,128]{2,1,0:T(8,128)(2,1)} %bitcast.13, f32[512,128]{1,0:T(8,128)} %start_h.1, bf16[28,256,256]{2,1,0:T(8,128)(2,1)} %bitcast.12, s32[28,256,256]{2,1,0:T(8,128)} %bitcast.11, s32[64,80]{1,0:T(8,128)} %bitcast.14, s32[5120]{0:T(1024)} %bitcast.15, s32[28]{0:T(128)} %bitcast.16, ...), custom_call_target="tpu_custom_call" | custom-call | tf_op jit(solution)/shard_map/pallas_call | solution.py:589
  91.5 1.5 %slice_bitcast_fusion = (f32[128,128]{1,0:T(8,128)}, f32[128,128]{1,0:T(8,128)}) fusion(f32[2,128,128]{2,1,0:T(8,128)} %shard_map.104), kind=kLoop, calls=%fused_computation | loop fusion | bytes 262144 | tf_op jit(solution)/shard_map/squeeze | solution.py:609

commit v4 on v3

--- a/solution.py
+++ b/solution.py
@@ -8,7 +8,7 @@
 from jax.sharding import PartitionSpec as P
 
 ITERS = 2
-GROUP = 4
+FIRST = 10
 LATER = 14
 
 ridge = 0.1
@@ -344,10 +344,10 @@
 
     def groups(step, vector, m, first, last, size):
         def one(g, carry):
-            group(step, vector, m, g * size, size)
+            group(step, vector, m, first + g * size, size)
             return carry
 
-        lax.fori_loop(first // size, last // size, one, 0)
+        lax.fori_loop(0, (last - first) // size, one, 0)
 
     def send_terms(step, m):
         at = pl.ds(m * slab, slab)
@@ -422,7 +422,7 @@
             hub_send.at[5], hub_recv.at[5], sibling, col,
         ).start()
     lax.fori_loop(middle, tail_tiles, tail_tile, 0)
-    groups(0, start_half, 0, hub_tiles, tiles, GROUP)
+    groups(0, start_half, 0, hub_tiles, tiles, FIRST)
     drain(hub_mine.at[pl.ds(0, n_cols // 2)], hub_recv.at[5])
     for n in range(hub_tiles):
         part = hub_all[hub_pick_s[n]]
@@ -430,9 +430,9 @@
             for c in range(2):
                 at = (2 * m + c) * part.shape[2]
                 factors[n, at : at + part.shape[2]] = part[c, m]
-    groups(0, start_half, 0, 0, hub_tiles, 2 * GROUP)
+    groups(0, start_half, 0, 0, hub_tiles, hub_tiles)
     send_terms(0, 0)
-    groups(0, start_half, 1, 0, tiles, LATER // 2)
+    groups(0, start_half, 1, 0, tiles, LATER)
     send_terms(0, 1)
 
     def reduce_terms(step):

time: 93.4 us -> 92.4 us (0.989)
  Pallas kernels: 90.9 us -> 89.9 us
    pallas_call x1, Pallas kernels: 90.9 us -> 89.9 us  [per_device(): pl.pallas_call(functools.partial(kernel, dims), out_shape=jax.ShapeDtypeS...]
where the time goes in v4:
time: 92.4 us; the launch traced here: 92.1 us
  Pallas kernels  89.9 us (97%)
  local copies, waits for them, and re-layouts  1.53 us (2%)
    pallas_call x1, Pallas kernels, per_device(): pl.pallas_call(functools.partial(kernel, dims), out_shape=jax.ShapeDtypeS...  89.9 us

profile of v4, /device:TPU:8, one launch (start us, length us, event | category | flops | bytes accessed | tf_op | source)
XLA Modules:
  0.0 92.1 jit_solution(10201323584677906674)
XLA Ops:
  0.6 89.9 %shard_map.104 = f32[2,128,128]{2,1,0:T(8,128)} custom-call(bf16[8,256,128]{2,1,0:T(8,128)(2,1)} %bitcast.13, f32[512,128]{1,0:T(8,128)} %start_h.1, bf16[28,256,256]{2,1,0:T(8,128)(2,1)} %bitcast.12, s32[28,256,256]{2,1,0:T(8,128)} %bitcast.11, s32[64,80]{1,0:T(8,128)} %bitcast.14, s32[5120]{0:T(1024)} %bitcast.15, s32[28]{0:T(128)} %bitcast.16, ...), custom_call_target="tpu_custom_call" | custom-call | tf_op jit(solution)/shard_map/pallas_call | solution.py:589
  90.5 1.5 %slice_bitcast_fusion = (f32[128,128]{1,0:T(8,128)}, f32[128,128]{1,0:T(8,128)}) fusion(f32[2,128,128]{2,1,0:T(8,128)} %shard_map.104), kind=kLoop, calls=%fused_computation | loop fusion | bytes 262144 | tf_op jit(solution)/shard_map/squeeze | solution.py:609
